TPU v7x, 128 devices: a whole 4x4x4 slice. The times are simulated.
128 devices in a mesh: layer: 8 (over x, z_hi), feat: 16 (over z_lo, y, core).
Axes of the slice: x: 4, y: 4, z: 4 (z_hi: 2, z_lo: 2; z = z_hi * 2 + z_lo), core: 2. Of those that a mesh axis runs over, the one named last changes fastest.
Arguments:
- sources: bfloat16 [2, 384, 4608], P(None, 'feat'), may hold values from -6 to 6
- targets: bfloat16 [4, 384, 4608], P(None, 'feat'), may hold values from -6 to 6
- blocks: bfloat16 [8, 32768, 4608], P('layer', 'feat'), may hold values from -0.09375 to 0.09375
- enc_bias: float32 [2, 32768], P(None, 'feat'), may hold values from -4 to 4
- token_code: int32 [2, 384], replicated, may hold values from 1 to 250
- feature_threshold_code: int32 [2, 32768], P(None, 'feat'), may hold values from 1 to 250
- dec_map: int32 [6], replicated, may hold values from 0 to 5, each once
Outputs:
- recon_error: float32 [4, 384, 4608], P(None, 'feat')
- pre_grads: bfloat16 [2, 384, 32768], P(None, 'layer', 'feat')
Inputs may be any that keep to these rules, and one draw needn't show every extreme that they name: `dec_map`: each pair number 0 to 5 stands once.
All inputs are finite; a program needn't handle non-finite values.
Results may differ from a plain program's by a relative error of at most 0.02.
Values may be sent and summed in bfloat16 or wider, within the bound.
A program may use at most 128 MiB of HBM per device.

v0:
```python
import jax
import jax.numpy as jnp
from jax import lax
from jax.sharding import PartitionSpec as P

K = 3


def broadcast(x, axis, root):
    mine = lax.axis_index(axis) == root
    return lax.psum(jnp.where(mine, x, jnp.zeros_like(x)), axis)


def active_feature_mask(token_row_block, feature_row_block):
    return (token_row_block[..., :, None] * feature_row_block[..., None, :] % 251 < 40).astype(
        jnp.float32
    )


def body(sources, targets, blocks, enc_bias, token_code, feature_threshold_code, dec_map):
    sources_n = sources.shape[0]
    targets_n = targets.shape[0]
    tokens_all = token_code.shape[1]
    weight = blocks[0]
    feat_cols = weight.shape[0]
    member = lax.axis_index("layer")
    encoder = member < sources_n
    slot_index = jnp.clip(member - sources_n, 0, sources_n * K - 1)
    pair = dec_map[slot_index]
    source_of = pair // K
    target_of = source_of + pair % K
    own_source = jnp.minimum(member, sources_n - 1)
    own_rows = lax.dynamic_index_in_dim(sources, own_source, 0, keepdims=False)
    own_bias = lax.dynamic_index_in_dim(enc_bias, own_source, 0, keepdims=False)
    contract_last = (((1,), (1,)), ((), ()))
    piece = lax.all_gather(own_rows, "feat", axis=0, tiled=True)
    pre = (
        lax.cond(
            encoder,
            lambda: lax.dot_general(
                piece, weight, contract_last, preferred_element_type=jnp.float32
            ),
            lambda: jnp.zeros((piece.shape[0], feat_cols), jnp.float32),
        )
        + own_bias
    )
    local_gate_values = active_feature_mask(
        lax.dynamic_index_in_dim(token_code, own_source, 0, keepdims=False),
        lax.dynamic_index_in_dim(feature_threshold_code, own_source, 0, keepdims=False),
    )
    feats = (pre * local_gate_values).astype(jnp.bfloat16)
    chosen = jnp.zeros_like(feats)
    for source in range(sources_n):
        arrived = broadcast(feats, "layer", source)
        chosen = jnp.where(source_of == source, arrived, chosen)
    count = lax.axis_size("feat") * targets.shape[1]
    picked = chosen
    shares = lax.psum_scatter(
        lax.cond(
            encoder,
            lambda: jnp.zeros((count, weight.shape[1]), jnp.float32),
            lambda: jnp.dot(picked, weight, preferred_element_type=jnp.float32),
        ).astype(jnp.bfloat16),
        "feat",
        scatter_dimension=0,
        tiled=True,
    ).astype(jnp.float32)
    placed = jnp.where(encoder, 0.0, 1.0) * (jnp.arange(targets_n) == target_of).astype(jnp.float32)
    recon = lax.psum((placed[:, None, None] * shares[None]).astype(jnp.bfloat16), "layer").astype(
        jnp.float32
    )
    recon_error = recon - targets.astype(jnp.float32)
    error_low = lax.dynamic_index_in_dim(recon_error, target_of, 0, keepdims=False).astype(
        jnp.bfloat16
    )
    against_piece = lax.all_gather(error_low, "feat", axis=0, tiled=True)
    grads = lax.cond(
        encoder,
        lambda: jnp.zeros((against_piece.shape[0], feat_cols), jnp.float32),
        lambda: lax.dot_general(
            against_piece, weight, contract_last, preferred_element_type=jnp.float32
        ),
    )
    source_weight = jnp.where(encoder, 0.0, 1.0) * (jnp.arange(sources_n) == source_of).astype(
        jnp.float32
    )
    terms = source_weight[:, None, None] * grads[None]
    rows_own = tokens_all // lax.axis_size("layer")
    total = lax.psum(terms.astype(jnp.bfloat16), "layer").astype(jnp.float32)
    mine = lax.dynamic_slice_in_dim(total, member * rows_own, rows_own, 1)
    threshold_codes = lax.dynamic_slice_in_dim(token_code, member * rows_own, rows_own, 1)
    gate_row_block = active_feature_mask(threshold_codes, feature_threshold_code)
    return (recon_error, (mine * gate_row_block).astype(jnp.bfloat16))


def solution(mesh):
    return jax.shard_map(
        body,
        mesh=mesh,
        in_specs=(
            P(None, "feat", None),
            P(None, "feat", None),
            P("layer", "feat", None),
            P(None, "feat"),
            P(),
            P(None, "feat"),
            P(),
        ),
        out_specs=(P(None, "feat", None), P(None, "layer", "feat")),
        check_vma=False,
    )
```

profile of v0, /device:TPU:1, one launch (start us, length us, event | category | flops | bytes accessed | tf_op | source)
XLA Modules:
  0.0 595.5 jit_solution(5363270678636075222)
XLA Ops:
  7.2 0.0 copy-start
  7.2 0.0 all-gather.5.cloned.1.call-start
  7.2 1.0 copy-done
  8.2 0.7 constant_dynamic-slice_fusion.2
  8.9 0.0 all-gather.5.cloned.1.call-update
  8.9 0.0 all-reduce.9.cloned.1.call-start
  9.0 0.7 fusion.13
  9.7 0.7 constant_dynamic-slice_fusion.3
  10.4 0.7 constant_dynamic-slice_fusion.1
  11.1 39.4 %all-gather.5.cloned.1.call-done = bf16[1,384,4608]{2,1,0:T(8,128)(2,1)} async-done(((bf16[1,24,4608]{2,1,0:T(8,128)(2,1)}), bf16[1,384,4608]{2,1,0:T(8,128)(2,1)}) %all-gather.5.cloned.1.call-update) | async-done | bytes 3538960 | tf_op jit(solution)/shard_map/all_gather | solution.py:36
  50.5 13.5 %conditional.3 = (f32[384,2048]{1,0:T(8,128)}) conditional(s32[]{:T(128)} %convert_element_type.42, () %tuple.26, (bf16[384,4608]{1,0:T(8,128)(2,1)}, bf16[2048,4608]{1,0:T(8,128)(2,1)}) %tuple.56), branch_computations={%region_0.1_spmd, %region_1.2_spmd} | conditional | flops 7247757312 | bytes 25559048 | solution.py:38
  50.5 13.5 %fusion.14 = f32[384,2048]{1,0:T(8,128)} fusion(bf16[384,4608]{1,0:T(8,128)(2,1)} %get-tuple-element.36, bf16[2048,4608]{1,0:T(8,128)(2,1)} %get-tuple-element.37), kind=kOutput, calls=%fused_computation.33 | convolution fusion | flops 7247757312 | bytes 25559040 | tf_op jit(solution)/shard_map/cond/branch_1_fun/dot_general | solution.py:40
  64.1 4.6 broadcast_select_fusion
  68.7 0.0 copy-start.4
  68.7 1.3 broadcast_select_fusion.1
  70.0 0.0 all-reduce.9.cloned.1.call-update
  70.0 0.0 reduce-scatter.2.cloned.1.call-start
  70.0 0.0 copy-done.4
  70.0 0.6 dynamic_slice.29
  72.6 141.3 %all-reduce.9.cloned.1.call-done = (bf16[384,2048]{1,0:T(8,128)(2,1)}, bf16[384,2048]{1,0:T(8,128)(2,1)}) async-done(((bf16[384,2048]{1,0:T(8,128)(2,1)}, bf16[384,2048]{1,0:T(8,128)(2,1)}), (bf16[384,2048]{1,0:T(8,128)(2,1)}, bf16[384,2048]{1,0:T(8,128)(2,1)})) %all-reduce.9.cloned.1.call-update) | async-done | bytes 3145744 | tf_op jit(solution)/shard_map/psum | solution.py:11
  213.9 0.2 broadcast.58
  214.1 2.0 conditional.4
  214.1 2.0 broadcast.49
  216.1 0.0 copy-start.2
  216.1 0.0 reduce-scatter.2.cloned.1.call-update
  216.1 0.0 all-reduce.5.cloned.1.call-start
  216.2 76.3 %reduce-scatter.2.cloned.1.call-done = bf16[24,4608]{1,0:T(8,128)(2,1)} async-done(((bf16[384,4608]{1,0:T(8,128)(2,1)}), bf16[24,4608]{1,0:T(8,128)(2,1)}) %reduce-scatter.2.cloned.1.call-update) | async-done | bytes 221200 | tf_op jit(solution)/shard_map/reduce_scatter | solution.py:58
  292.5 1.0 convert_element_type.45
  293.4 1.1 multiply_convert_fusion.1
  294.5 0.0 all-reduce.5.cloned.1.call-update
  294.5 0.0 all-gather.7.cloned.1.call-start
  294.6 86.5 %all-reduce.5.cloned.1.call-done = bf16[4,24,4608]{2,1,0:T(8,128)(2,1)} async-done(((bf16[4,24,4608]{2,1,0:T(8,128)(2,1)}), bf16[4,24,4608]{2,1,0:T(8,128)(2,1)}) %all-reduce.5.cloned.1.call-update) | async-done | bytes 884752 | tf_op jit(solution)/shard_map/psum | solution.py:69
  381.1 0.0 copy-done.2
  381.1 1.4 convert_subtract_fusion
  382.5 0.0 copy-start.1
  382.5 0.8 dynamic-slice_convert_fusion
  383.3 0.0 all-gather.7.cloned.1.call-update
  383.3 0.0 all-reduce.7.cloned.1.call-start
  383.3 39.6 %all-gather.7.cloned.1.call-done = bf16[1,384,4608]{2,1,0:T(8,128)(2,1)} async-done(((bf16[1,24,4608]{2,1,0:T(8,128)(2,1)}), bf16[1,384,4608]{2,1,0:T(8,128)(2,1)}) %all-gather.7.cloned.1.call-update) | async-done | bytes 3538960 | tf_op jit(solution)/shard_map/all_gather | solution.py:76
  422.9 0.0 copy-done.1
  422.9 2.1 conditional.5
  422.9 2.1 broadcast.50
  425.0 4.3 multiply_convert_fusion
  429.3 0.0 copy-start.3
  429.3 0.0 all-reduce.7.cloned.1.call-update
  429.3 0.8 constant_dynamic-slice_fusion
  430.1 156.3 %all-reduce.7.cloned.1.call-done = bf16[2,384,2048]{2,1,0:T(8,128)(2,1)} async-done(((bf16[2,384,2048]{2,1,0:T(8,128)(2,1)}), bf16[2,384,2048]{2,1,0:T(8,128)(2,1)}) %all-reduce.7.cloned.1.call-update) | async-done | bytes 3145744 | tf_op jit(solution)/shard_map/psum | solution.py:89
  586.3 0.0 copy-done.3
  586.3 2.3 select_convert_fusion.1
  (2 shorter events, 0.0 us)
Async XLA Ops:
  7.2 1.0 copy-start
  7.2 43.4 %all-gather.5.cloned.1.call-start = ((), (), s32[]{:S(2)}) async-start(), calls=%async_computation.4 | async-start | bytes 3760128 | tf_op jit(solution)/shard_map/all_gather | solution.py:36
  8.9 205.0 %all-reduce.9.cloned.1.call-start = ((), (), s32[]{:S(2)}) async-start(), calls=%async_computation.6 | async-start | bytes 6291456 | tf_op jit(solution)/shard_map/psum | solution.py:11
  68.7 1.4 copy-start.4
  70.0 222.5 %reduce-scatter.2.cloned.1.call-start = ((), (), s32[]{:S(2)}) async-start(), calls=%async_computation.1 | async-start | bytes 3760128 | tf_op jit(solution)/shard_map/reduce_scatter | solution.py:58
  216.1 165.0 %copy-start.2 = (bf16[4,24,4608]{2,1,0:T(8,128)(2,1)S(1)}, bf16[4,24,4608]{2,1,0:T(8,128)(2,1)}, u32[]{:S(2)}) copy-start(bf16[4,24,4608]{2,1,0:T(8,128)(2,1)} %param.14) | copy-start | bytes 2654212
  216.1 165.0 %all-reduce.5.cloned.1.call-start = ((), (), s32[]{:S(2)}) async-start(), calls=%async_computation.2 | async-start | bytes 1769472 | tf_op jit(solution)/shard_map/psum | solution.py:69
  294.5 128.4 %all-gather.7.cloned.1.call-start = ((), (), s32[]{:S(2)}) async-start(), calls=%async_computation.5 | async-start | bytes 3760128 | tf_op jit(solution)/shard_map/all_gather | solution.py:76
  382.5 40.5 %copy-start.1 = (f32[4,24,4608]{2,1,0:T(8,128)}, f32[4,24,4608]{2,1,0:T(8,128)S(1)}, u32[]{:S(2)}) copy-start(f32[4,24,4608]{2,1,0:T(8,128)S(1)} %convert_subtract_fusion) | copy-start | bytes 5308420
  383.3 203.0 %all-reduce.7.cloned.1.call-start = ((), (), s32[]{:S(2)}) async-start(), calls=%async_computation.3 | async-start | bytes 6291456 | tf_op jit(solution)/shard_map/psum | solution.py:89
  429.3 157.0 %copy-start.3 = (s32[2,2048]{1,0:T(2,128)S(1)}, s32[2,2048]{1,0:T(2,128)}, u32[]{:S(2)}) copy-start(s32[2,2048]{1,0:T(2,128)} %param.18) | copy-start | bytes 49156
Sparse Core Ops, SparseCore 0:
  10.3 40.2 all-gather.4
  70.1 143.7 all-reduce.8
  216.3 76.1 reduce-scatter.1
  295.4 85.5 all-reduce.4
  383.4 39.4 all-gather.6
  429.4 156.8 all-reduce.6
where the time goes:
time: 599 us; the launch traced here: 595 us
  waiting for transfers between devices  539 us (90%)
  between operations  16.2 us (3%)
  other arithmetic  15.9 us (3%)
  matrix products  13.5 us (2%)
  local copies, waits for them, and re-layouts  10.2 us (2%)
    psum x1, waiting for transfers between devices, body(): total = lax.psum(terms.astype(jnp.bfloat16), 'layer').astype(jnp.float32)  156 us
    psum x1, waiting for transfers between devices, broadcast(): return lax.psum(jnp.where(mine, x, jnp.zeros_like(x)), axis)  141 us
    psum x1, waiting for transfers between devices, body(): lax.psum((placed[:, None, None] * shares[None]).astype(jnp.bfloat16), 'la...  86.5 us
    reduce_scatter x1, waiting for transfers between devices, body(): lax.psum_scatter(lax.cond(encoder, lambda: jnp.zeros((count, weight.shape...  76.3 us
    all_gather x1, waiting for transfers between devices, body(): against_piece = lax.all_gather(error_low, 'feat', axis=0, tiled=True)  39.6 us
    all_gather x1, waiting for transfers between devices, body(): piece = lax.all_gather(own_rows, 'feat', axis=0, tiled=True)  39.4 us
    dot_general x1, matrix products, body(): lax.dot_general(piece, weight, contract_last, preferred_element_type=jnp....  13.5 us
  transfers between devices with their start and end apart: 6, of which 6 were waited for; matrix products, arithmetic and copies ran while one was open for 1% of the time, Pallas kernels for 0%

commit v1 on v0

v1 whole, which is shorter than its diff:
```python
import jax
import jax.numpy as jnp
from jax import lax
from jax.experimental import pallas as pl
from jax.experimental.pallas import tpu as pltpu
from jax.sharding import PartitionSpec as P

MESH = pl.DeviceIdType.MESH
F32 = jnp.float32
BF16 = jnp.bfloat16

ROWS = 48
HALF = 2304
WIDE = (1024, 1280)
COL = (0, 1024)
NCH = 8
CH = 256
HR = 192
CROSS0 = 3
FLAG = 3
LH = 1
ML = 6
GN = 4
GC = 512

NT = (((1,), (1,)), ((), ()))
PAIRS = ((0,), (1, 3), (2, 4), (5,))


def gate_of(tok, code):
    v = tok * code
    q = jnp.floor(v * (1.0 / 251.0))
    return (v - 251.0 * q) < 40.0


def kernel(
    dm, src, tgt, w_hbm, bias, tok, fc, err_out, pg_out,
    W, X0, X1, FB, acc, sx_send, sx, tg_send, tg, TK, FC,
    S0, S1, C0, C1, T0, T1, RZ0, RY1, V0, RY0, V1, RZ1, RL0, RL1, E0, E1, ER0, ER1, GS, GR,
    wsem, xsem, ags, agr, bs, br, fs, fcs, fr, cs, cr, ls, lr, es, er, gs, gr,
):
    layer = lax.axis_index("layer")
    feat = lax.axis_index("feat")
    x, h = layer // 2, layer % 2
    l, y, c = feat // 8, (feat // 2) % 4, feat % 2
    u = feat // 2
    o = 1 - c
    uz = (1 - l) * 4 + y
    X = (X0, X1)

    def dev(x=x, h=h, l=l, y=y, c=c):
        return (2 * x + h, (4 * l + y) * 2 + c)

    ys = [lax.rem(y + k, 4) for k in (1, 2, 3)]
    xs = [lax.rem(x + k, 4) for k in (1, 2, 3)]
    sib = dev(c=o)
    zp = dev(l=1 - l)
    cross = dev(h=1 - h)

    bar = pltpu.get_barrier_semaphore()
    peers = [sib, zp, cross]
    peers += [dev(y=a) for a in ys] + [dev(y=a, l=1 - l) for a in ys]
    peers += [dev(x=a) for a in xs] + [dev(x=a, h=1 - h) for a in xs]
    for p in peers:
        pl.semaphore_signal(bar, inc=1, device_id=p, device_id_type=MESH)

    wcp = [
        pltpu.make_async_copy(w_hbm.at[0, pl.ds(CH * k, CH)], W.at[pl.ds(CH * k, CH)], wsem.at[k])
        for k in range(NCH)
    ]
    for cp in wcp:
        cp.start()

    for s in range(2):
        TK[s] = jnp.transpose(jnp.broadcast_to(tok[s : s + 1, :].astype(F32), (128, 384)))
    FC[...] = fc[...].astype(F32)

    def rcopy(a, b, ssem, rsem, to, sends):
        cp = pltpu.make_async_remote_copy(
            src_ref=a, dst_ref=b, send_sem=ssem, recv_sem=rsem, device_id=to, device_id_type=MESH
        )
        cp.start()
        sends.append(cp)

    def arrived(b, rsem):
        pltpu.make_async_remote_copy(
            src_ref=b, dst_ref=b, send_sem=rsem, recv_sem=rsem, device_id=sib, device_id_type=MESH
        ).wait_recv()

    pl.semaphore_wait(bar, len(peers))

    def half_of(v, which):
        return jnp.where(which == 0, v[..., :HALF], v[..., HALF:])

    first = []
    own = pl.ds(pl.multiple_of(24 * c, 8), 24)
    for t in range(4):
        v = tgt[t].astype(F32)
        tg_send[t] = half_of(v, o)
        tg[t, own, :] = half_of(v, c)
    v = jnp.where(h == 0, src[0].astype(F32), src[1].astype(F32))
    sx_send[...] = half_of(v, o)
    sx[own, :] = half_of(v, c)
    rcopy(sx_send, sx.at[own, :], xsem.at[0], xsem.at[1], sib, first)
    rcopy(tg_send, tg.at[:, own, :], xsem.at[2], xsem.at[3], sib, first)
    other = pl.ds(pl.multiple_of(24 * o, 8), 24)
    arrived(sx.at[other, :], xsem.at[1])
    arrived(tg.at[:, other, :], xsem.at[3])
    for cp in first:
        cp.wait_send()

    def all_gather():
        sends = []
        n = [0]

        def send(p, b, to, rsem=None):
            r = X[p].at[c, b]
            rcopy(r, r, ags.at[n[0]], agr.at[p, b] if rsem is None else rsem, to, sends)
            n[0] += 1

        def both(p, b):
            send(p, b, sib, br.at[p, b])

        send(0, u, zp)
        for k in range(3):
            send(1, u, dev(y=ys[k]))
            send(0, u, dev(y=ys[k]))
        send(1, u, zp)
        both(0, u)
        both(1, u)
        arrived(X0.at[c, uz], agr.at[0, uz])
        for k in range(3):
            send(0, uz, dev(y=ys[k]))
        both(0, uz)
        for k in (0, 2, 1):
            b = l * 4 + ys[k]
            arrived(X1.at[c, b], agr.at[1, b])
            send(1, b, zp)
            both(1, b)
        for k in (0, 2, 1):
            b = l * 4 + ys[k]
            arrived(X0.at[c, b], agr.at[0, b])
            both(0, b)
        arrived(X1.at[c, uz], agr.at[1, uz])
        both(1, uz)
        for k in (0, 2, 1):
            b = (1 - l) * 4 + ys[k]
            arrived(X0.at[c, b], agr.at[0, b])
            both(0, b)
            arrived(X1.at[c, b], agr.at[1, b])
            both(1, b)
        for p in range(2):
            for b in range(8):
                arrived(X[p].at[o, b], br.at[p, b])
        for cp in sends:
            cp.wait_send()

    def against(rows):
        total = None
        for cc in range(2):
            for p in range(2):
                a = X[p][cc].reshape(384, WIDE[p])
                b = W[rows, cc * HALF + COL[p] : cc * HALF + COL[p] + WIDE[p]]
                d = lax.dot_general(a, b, NT, preferred_element_type=F32)
                total = d if total is None else total + d
        return total

    @pl.when(x == 0)
    def _():
        for p in range(2):
            X[p][c, u] = sx[:, COL[p] : COL[p] + WIDE[p]].astype(BF16)
        all_gather()
        line = (dev(x=1), dev(x=3))

        def chunk(k, _):
            rows = pl.ds(pl.multiple_of(k * CH, CH), CH)
            pltpu.make_async_copy(w_hbm.at[0, rows], W.at[rows], wsem.at[k]).wait()
            pre = against(rows) + bias[pl.ds(h, 1), rows]
            on = gate_of(jnp.concatenate([TK[h]] * 2, axis=1), FC[pl.ds(h, 1), rows])
            FB[h, k] = jnp.where(on, pre, 0.0).astype(BF16).reshape(2, HR, CH)
            junk = []
            for half in range(2):
                r = FB.at[h, k, half]
                rcopy(r, r, fs.at[h, k, half], fr.at[h, k, half], line[half], junk)

            @pl.when(k < CROSS0)
            def _():
                for half in range(2):
                    r = FB.at[h, k, half]
                    rcopy(r, r, fcs.at[k, half], fr.at[h, k, half], cross, junk)

            j = k - FLAG

            @pl.when((j >= 0) & (j < CROSS0))
            def _():
                for half in range(2):
                    r = FB.at[1 - h, j, half]
                    arrived(r, fr.at[1 - h, j, half])
                    rcopy(r, r, fs.at[1 - h, j, half], fr.at[1 - h, j, half], line[half], junk)

            return 0

        lax.fori_loop(0, NCH, chunk, 0)

        def drain(k, _):
            for half in range(2):
                r = FB.at[h, k, half]
                pltpu.make_async_remote_copy(r, r, fs.at[h, k, half], fr.at[h, k, half], line[half], MESH).wait_send()

                @pl.when(k < CROSS0)
                def _():
                    pltpu.make_async_remote_copy(r, r, fcs.at[k, half], fr.at[h, k, half], cross, MESH).wait_send()
                    q = FB.at[1 - h, k, half]
                    pltpu.make_async_remote_copy(q, q, fs.at[1 - h, k, half], fr.at[1 - h, k, half], line[half], MESH).wait_send()

            return 0

        lax.fori_loop(0, NCH, drain, 0)

    slot = jnp.maximum(layer - 2, 0)
    pair = dm[slot]
    mine_src = (pair >= 3).astype(jnp.int32)
    mine_tgt = pair - 2 * mine_src
    place = []
    for p in range(6):
        at = jnp.int32(0)
        for i in range(6):
            at = jnp.where(dm[i] == p, jnp.int32(i + 2), at)
        place.append(at)

    @pl.when(x > 0)
    def _():
        acc[...] = jnp.zeros_like(acc)
        nxt = (dev(x=lax.rem(x + 1, 4)), dev(x=lax.rem(x + 3, 4)))
        more = (x < 3, x > 1)
        lag = ((x - 1) * LH, (3 - x) * LH)

        def fwd(s, k, half):
            r = FB.at[s, k, half]
            return pltpu.make_async_remote_copy(r, r, fs.at[s, k, half], fr.at[s, k, half], nxt[half], MESH)

        def over(k, half):
            r = FB.at[h, k, half]
            return pltpu.make_async_remote_copy(r, r, fcs.at[k, half], fr.at[h, k, half], cross, MESH)

        def step(t, _):
            for half in range(2):
                k = t - lag[half]

                @pl.when((k >= 0) & (k < NCH))
                def _():
                    arrived(FB.at[h, k, half], fr.at[h, k, half])

                    @pl.when(more[half])
                    def _():
                        fwd(h, k, half).start()

                    @pl.when(k >= CROSS0)
                    def _():
                        over(k, half).start()

                j = k - FLAG

                @pl.when((j >= 0) & (j < CROSS0))
                def _():
                    arrived(FB.at[1 - h, j, half], fr.at[1 - h, j, half])

                    @pl.when(more[half])
                    def _():
                        fwd(1 - h, j, half).start()

            m = t - ML

            @pl.when((m >= 0) & (m < NCH))
            def _():
                @pl.when(m >= CROSS0)
                def _():
                    for half in range(2):
                        arrived(FB.at[1 - h, m, half], fr.at[1 - h, m, half])

                rows = pl.ds(pl.multiple_of(m * CH, CH), CH)
                pltpu.make_async_copy(w_hbm.at[0, rows], W.at[rows], wsem.at[m]).wait()
                a = jnp.where(mine_src == 0, FB[0, m], FB[1, m]).reshape(384, CH)
                for cc in range(2):
                    for n in range(3):
                        cols = slice(cc * HALF + n * 768, cc * HALF + (n + 1) * 768)
                        acc[cc, :, n * 768 : (n + 1) * 768] += jnp.dot(a, W[rows, cols], preferred_element_type=F32)

            return 0

        lax.fori_loop(0, NCH + ML, step, 0)

        def drain(k, _):
            for half in range(2):

                @pl.when(more[half])
                def _():
                    fwd(h, k, half).wait_send()

                    @pl.when(k < CROSS0)
                    def _():
                        fwd(1 - h, k, half).wait_send()

                @pl.when(k >= CROSS0)
                def _():
                    over(k, half).wait_send()

            return 0

        lax.fori_loop(0, NCH, drain, 0)

        sends = []
        S, C, T = (S0, S1), (C0, C1), (T0, T1)
        for p in range(2):
            cols = slice(COL[p], COL[p] + WIDE[p])
            S[p][...] = acc[o, :, cols].astype(BF16).reshape(8, ROWS, WIDE[p])
            rcopy(S[p], C[p], cs.at[p], cr.at[p], sib, sends)
        for p in range(2):
            cols = slice(COL[p], COL[p] + WIDE[p])
            arrived(C[p], cr.at[p])
            T[p][...] = (acc[c, :, cols] + C[p][...].astype(F32).reshape(384, WIDE[p])).astype(BF16).reshape(8, ROWS, WIDE[p])
            if p == 0:
                rcopy(T0.at[pl.ds((1 - l) * 4, 4)], RZ0, cs.at[2], cr.at[2], zp, sends)
        for k in range(3):
            for q in range(2):
                rcopy(T1.at[q * 4 + ys[k]], RY1.at[2 - k, q], cs.at[3 + 2 * k + q], cr.at[3 + 2 * (2 - k) + q], dev(y=ys[k]), sends)
        arrived(RZ0, cr.at[2])
        V0[...] = (T0[pl.ds(l * 4, 4)].astype(F32) + RZ0[...].astype(F32)).astype(BF16)
        for k in range(3):
            rcopy(V0.at[ys[k]], RY0.at[2 - k], cs.at[9 + k], cr.at[9 + 2 - k], dev(y=ys[k]), sends)
        for k in range(3):
            for q in range(2):
                arrived(RY1.at[k, q], cr.at[3 + 2 * k + q])
        total = [
            sum([RY1[k, q].astype(F32) for k in range(3)], T1[q * 4 + y].astype(F32)) for q in range(2)
        ]
        V1[...] = jnp.where(l == 0, total[1], total[0]).astype(BF16)
        rcopy(V1, RZ1, cs.at[12], cr.at[12], zp, sends)
        mine1 = jnp.where(l == 0, total[0], total[1])
        for k in range(3):
            arrived(RY0.at[k], cr.at[9 + k])
        RL0[layer] = sum([RY0[k].astype(F32) for k in range(3)], V0[y].astype(F32)).astype(BF16)
        arrived(RZ1, cr.at[12])
        RL1[layer] = (mine1 + RZ1[...].astype(F32)).astype(BF16)
        for cp in sends:
            cp.wait_send()

    def lcopy(p, m, ssem, to):
        r = (RL0, RL1)[p].at[m]
        return pltpu.make_async_remote_copy(r, r, ssem, lr.at[p, m], to, MESH)

    def lwait(p, m):
        arrived((RL0, RL1)[p].at[m], lr.at[p, m])

    ops = []

    @pl.when(x > 0)
    def _():
        lcopy(0, layer, ls.at[0], cross).start()
        for k in range(3):
            lcopy(1, layer, ls.at[1 + k], dev(x=xs[k])).start()
            lcopy(0, layer, ls.at[4 + k], dev(x=xs[k])).start()
        lcopy(1, layer, ls.at[7], cross).start()
        m = 2 * x + 1 - h
        lwait(0, m)
        for k in range(3):
            lcopy(0, m, ls.at[8 + k], dev(x=xs[k])).start()

    for k in (0, 2, 1):
        m = 2 * xs[k] + h

        @pl.when(xs[k] > 0)
        def _():
            lwait(1, m)
            lcopy(1, m, ls.at[11 + k], cross).start()

    for k in (0, 2, 1):

        @pl.when(xs[k] > 0)
        def _():
            lwait(0, 2 * xs[k] + h)
            lwait(0, 2 * xs[k] + 1 - h)
            lwait(1, 2 * xs[k] + 1 - h)

    @pl.when(x > 0)
    def _():
        lwait(1, 2 * x + 1 - h)

    for p, (RL, E) in enumerate(((RL0, E0), (RL1, E1))):
        for t in range(4):
            v = RL[place[PAIRS[t][0]]].astype(F32)
            for q in PAIRS[t][1:]:
                v = v + RL[place[q]].astype(F32)
            E[t] = v - tg[t, :, COL[p] : COL[p] + WIDE[p]]

    esends = []
    rcopy(E0.at[:, other, :], ER0, es.at[0], er.at[0], sib, esends)
    rcopy(E1.at[:, other, :], ER1, es.at[1], er.at[1], sib, esends)

    @pl.when(x > 0)
    def _():
        X0[c, u] = E0[mine_tgt].astype(BF16)
        X1[c, u] = E1[mine_tgt].astype(BF16)
        all_gather()

        def chunk(n, _):
            rows = pl.ds(pl.multiple_of(n * GC, GC), GC)
            v = against(rows).astype(BF16).reshape(8, ROWS, GC)
            GS[n] = v
            GR[layer, n] = GS[n, layer]
            for k in range(1, 8):
                m = lax.rem(layer + k, 8)
                pltpu.make_async_remote_copy(
                    GS.at[n, m], GR.at[layer, n], gs.at[n, k], gr.at[layer, n], (m, feat), MESH
                ).start()
            return 0

        lax.fori_loop(0, GN, chunk, 0)

    arrived(ER0, er.at[0])
    arrived(ER1, er.at[1])
    for p, (E, ER) in enumerate(((E0, ER0), (E1, ER1))):
        for cc in range(2):
            cols = slice(cc * HALF + COL[p], cc * HALF + COL[p] + WIDE[p])
            err_out[:, :, cols] = jnp.where(c == cc, E[:, own, :], ER[...])

    for m in range(2, 8):

        @pl.when(layer != m)
        def _():
            for n in range(GN):
                arrived(GR.at[m, n], gr.at[m, n])

    rows = pl.ds(pl.multiple_of(ROWS * layer, 8), ROWS)
    for s in range(2):
        for n in range(GN):
            v = GR[place[3 * s], n].astype(F32)
            for q in (1, 2):
                v = v + GR[place[3 * s + q], n].astype(F32)
            cols = slice(GC * n, GC * (n + 1))
            on = gate_of(jnp.concatenate([TK[s, rows, :]] * (GC // 128), axis=1), FC[s : s + 1, cols])
            pg_out[s, :, cols] = jnp.where(on, v, 0.0).astype(BF16)

    for cp in esends:
        cp.wait_send()

    @pl.when(x > 0)
    def _():
        lcopy(0, layer, ls.at[0], cross).wait_send()
        for k in range(3):
            lcopy(1, layer, ls.at[1 + k], dev(x=xs[k])).wait_send()
            lcopy(0, layer, ls.at[4 + k], dev(x=xs[k])).wait_send()
            lcopy(0, 2 * x + 1 - h, ls.at[8 + k], dev(x=xs[k])).wait_send()
        lcopy(1, layer, ls.at[7], cross).wait_send()

        def drain(n, _):
            for k in range(1, 8):
                m = lax.rem(layer + k, 8)
                pltpu.make_async_remote_copy(
                    GS.at[n, m], GR.at[layer, n], gs.at[n, k], gr.at[layer, n], (m, feat), MESH
                ).wait_send()
            return 0

        lax.fori_loop(0, GN, drain, 0)

    for k in range(3):

        @pl.when(xs[k] > 0)
        def _():
            lcopy(1, 2 * xs[k] + h, ls.at[11 + k], cross).wait_send()


def body(sources, targets, blocks, enc_bias, token_code, feature_threshold_code, dec_map):
    vm = pl.BlockSpec(memory_space=pltpu.VMEM)
    V = pltpu.VMEM
    D = pltpu.SemaphoreType.DMA
    w0, w1 = WIDE
    return pl.pallas_call(
        kernel,
        out_shape=(
            jax.ShapeDtypeStruct((4, 24, 4608), F32),
            jax.ShapeDtypeStruct((2, 48, 2048), BF16),
        ),
        in_specs=[pl.BlockSpec(memory_space=pltpu.SMEM), vm, vm, pl.BlockSpec(memory_space=pl.ANY), vm, vm, vm],
        out_specs=(vm, vm),
        scratch_shapes=[
            V((2048, 4608), BF16),
            V((2, 8, ROWS, w0), BF16),
            V((2, 8, ROWS, w1), BF16),
            V((2, NCH, 2, HR, CH), BF16),
            V((2, 384, HALF), F32),
            V((24, HALF), F32),
            V((ROWS, HALF), F32),
            V((4, 24, HALF), F32),
            V((4, ROWS, HALF), F32),
            V((2, 384, 128), F32),
            V((2, 2048), F32),
            V((8, ROWS, w0), BF16),
            V((8, ROWS, w1), BF16),
            V((8, ROWS, w0), BF16),
            V((8, ROWS, w1), BF16),
            V((8, ROWS, w0), BF16),
            V((8, ROWS, w1), BF16),
            V((4, ROWS, w0), BF16),
            V((3, 2, ROWS, w1), BF16),
            V((4, ROWS, w0), BF16),
            V((3, ROWS, w0), BF16),
            V((ROWS, w1), BF16),
            V((ROWS, w1), BF16),
            V((8, ROWS, w0), BF16),
            V((8, ROWS, w1), BF16),
            V((4, ROWS, w0), F32),
            V((4, ROWS, w1), F32),
            V((4, 24, w0), F32),
            V((4, 24, w1), F32),
            V((GN, 8, ROWS, GC), BF16),
            V((8, GN, ROWS, GC), BF16),
            D((NCH,)),
            D((4,)),
            D((32,)),
            D((2, 8)),
            D((2,)),
            D((2, 8)),
            D((2, NCH, 2)),
            D((NCH, 2)),
            D((2, NCH, 2)),
            D((13,)),
            D((13,)),
            D((14,)),
            D((2, 8)),
            D((2,)),
            D((2,)),
            D((GN, 8)),
            D((8, GN)),
        ],
        compiler_params=pltpu.CompilerParams(
            collective_id=1, has_side_effects=True, vmem_limit_bytes=61 * 2**20
        ),
        name="transcoder",
    )(dec_map, sources, targets, blocks, enc_bias, token_code, feature_threshold_code)


def solution(mesh):
    return jax.shard_map(
        body,
        mesh=mesh,
        in_specs=(
            P(None, "feat", None),
            P(None, "feat", None),
            P("layer", "feat", None),
            P(None, "feat"),
            P(),
            P(None, "feat"),
            P(),
        ),
        out_specs=(P(None, "feat", None), P(None, "layer", "feat")),
        check_vma=False,
    )
```

time: 599 us -> 165 us (0.28)
  waiting for transfers between devices: 539 us -> 0 us
  Pallas kernels: 0 us -> 160 us
  other arithmetic: 15.9 us -> 0 us
  between operations: 16.2 us -> 0.65 us
  matrix products: 13.5 us -> 0 us
  local copies, waits for them, and re-layouts: 10.2 us -> 3.6 us
    psum x3 -> x0, waiting for transfers between devices: 384 us -> none  [the longest x1 156 us: body(): total = lax.psum(terms.astype(jnp.bfloat16), 'layer').astype(jnp.float32)]
    pallas_call x0 -> x1, Pallas kernels: none -> 160 us  [body(): pl.pallas_call(kernel, out_shape=(jax.ShapeDtypeStruct((4, 24, 4608), F32...]
    all_gather x2 -> x0, waiting for transfers between devices: 79 us -> none  [the longest x1 39.6 us: body(): against_piece = lax.all_gather(error_low, 'feat', axis=0, tiled=True)]
    reduce_scatter x1 -> x0, waiting for transfers between devices: 76.3 us -> none  [body(): lax.psum_scatter(lax.cond(encoder, lambda: jnp.zeros((count, weight.shape...]
    dot_general x1 -> x0, matrix products: 13.5 us -> none  [body(): lax.dot_general(piece, weight, contract_last, preferred_element_type=jnp....]
    convert_element_type x4 -> x0, other arithmetic: 8.62 us -> none  [the longest x1 4.27 us: body(): total = lax.psum(terms.astype(jnp.bfloat16), 'layer').astype(jnp.float32)]
  transfers between devices with their start and end apart: 6 -> 0, of which waited for: 6 -> 0; matrix products, arithmetic and copies ran while one was open for 1% -> 0% of each run, Pallas kernels for 0% -> 0%
where the time goes in v1:
time: 165 us; the launch traced here: 164 us
  Pallas kernels  160 us (97%)
  local copies, waits for them, and re-layouts  3.6 us (2%)
    pallas_call x1, Pallas kernels, body(): pl.pallas_call(kernel, out_shape=(jax.ShapeDtypeStruct((4, 24, 4608), F32...  160 us
    unnamed x4, local copies, waits for them, and re-layouts  3.6 us

profile of v1, /device:TPU:1, one launch (start us, length us, event | category | flops | bytes accessed | tf_op | source)
XLA Modules:
  0.0 164.1 jit_solution(6947402600813372977)
XLA Ops:
  0.6 159.8 %transcoder.1 = (f32[4,24,4608]{2,1,0:T(8,128)}, bf16[2,48,2048]{2,1,0:T(8,128)(2,1)}) custom-call(s32[6]{0:T(128)} %dm.1, bf16[2,24,4608]{2,1,0:T(8,128)(2,1)} %src.1, bf16[4,24,4608]{2,1,0:T(8,128)(2,1)} %tgt.1, bf16[1,2048,4608]{2,1,0:T(8,128)(2,1)} %w_hbm.1, f32[2,2048]{1,0:T(2,128)} %bias.1, s32[2,384]{1,0:T(2,128)} %tok.1, s32[2,2048]{1,0:T(2,128)} %fc.1), custom_call_target="tpu_custom_call" | custom-call | tf_op jit(solution)/shard_map/transcoder/pallas_call | solution.py:478
  160.5 0.0 copy-start
  160.5 2.8 %copy.11 = f32[4,24,4608]{2,1,0:T(8,128)} copy(f32[4,24,4608]{2,1,0:T(8,128)} %get-tuple-element.4) | data formatting | bytes 3538944
  163.3 0.0 copy-done
  163.3 0.7 copy.12
Async XLA Ops:
  160.5 2.9 %copy-start = (bf16[2,48,2048]{2,1,0:T(8,128)(2,1)S(1)}, bf16[2,48,2048]{2,1,0:T(8,128)(2,1)}, u32[]{:S(2)}) copy-start(bf16[2,48,2048]{2,1,0:T(8,128)(2,1)} %get-tuple-element.5) | copy-start | bytes 1179652

commit v2 on v0

v2 whole, which is shorter than its diff:
```python
import jax
import jax.numpy as jnp
from jax import lax
from jax.experimental import pallas as pl
from jax.experimental.pallas import tpu as pltpu
from jax.sharding import PartitionSpec as P

MESH = pl.DeviceIdType.MESH
F32 = jnp.float32
BF16 = jnp.bfloat16

ROWS = 48
HALF = 2304
GRP = 3
GW = 768
MID = 384
NCH = 8
CH = 256
SUB = 96
STEPS = 2 * NCH
CROSS0 = 3
FLAG = 5
LH = 3
ML = 12
GN = 8
GC = 256
GLAG = 3
ZG = 2

NT = (((1,), (1,)), ((), ()))
PAIRS = ((0,), (1, 3), (2, 4), (5,))


def gate_of(tok, code):
    v = tok * code
    q = jnp.floor(v * (1.0 / 251.0))
    return (v - 251.0 * q) < 40.0


def kernel(
    dm, src, tgt, w_hbm, bias, tok, fc, rec_out, pg_out,
    W, X, XO, FB, acc, sx_send, sx, tg_send, tg, TK, FC,
    S, C, T, RY, V1, RZ, R0, R1, R2, E, ER, GS, GA, GO, GC_, GZ,
    wsem, xsem, ags, agr, br, fs, fcs, fr, ss, sr, ys_s, ys_r, zs, zr, ls, lr, es, er, gs, gr, gzs, gzr,
):
    layer = lax.axis_index("layer")
    feat = lax.axis_index("feat")
    x, h = layer // 2, layer % 2
    l, y, c = feat // 8, (feat // 2) % 4, feat % 2
    o = 1 - c
    RL = (R0, R1, R2)

    def dev(x=x, h=h, l=l, y=y, c=c):
        return (2 * x + h, (4 * l + y) * 2 + c)

    ys = [lax.rem(y + k, 4) for k in (1, 2, 3)]
    xs = [lax.rem(x + k, 4) for k in (1, 2, 3)]
    sib = dev(c=o)
    zp = dev(l=1 - l)
    zo = dev(h=1 - h, l=1 - l)
    cross = dev(h=1 - h)

    def copy(a, b, ssem, rsem, to):
        return pltpu.make_async_remote_copy(
            src_ref=a, dst_ref=b, send_sem=ssem, recv_sem=rsem, device_id=to, device_id_type=MESH
        )

    def rcopy(a, b, ssem, rsem, to, sends):
        cp = copy(a, b, ssem, rsem, to)
        cp.start()
        sends.append(cp)

    def arrived(b, rsem):
        copy(b, b, rsem, rsem, sib).wait_recv()

    def half_of(v, which):
        return jnp.where(which == 0, v[..., :HALF], v[..., HALF:])

    own = pl.ds(pl.multiple_of(24 * c, 8), 24)
    other = pl.ds(pl.multiple_of(24 * o, 8), 24)

    def enter():
        bar = pltpu.get_barrier_semaphore()
        peers = [sib, zp, zo, cross] + [dev(y=a) for a in ys]
        peers += [dev(x=a) for a in xs] + [dev(x=a, h=1 - h) for a in xs]
        for p in peers:
            pl.semaphore_signal(bar, inc=1, device_id=p, device_id_type=MESH)
        for k in range(NCH):
            rows = pl.ds(CH * k, CH)
            pltpu.make_async_copy(w_hbm.at[0, rows], W.at[rows], wsem.at[k]).start()
        v = src[...].astype(F32)
        sx_send[...] = half_of(v, o)
        sx[:, own, :] = half_of(v, c)
        pl.semaphore_wait(bar, len(peers))

    def sources_in(sends):
        rcopy(sx_send, sx.at[:, own, :], xsem.at[0], xsem.at[1], sib, sends)
        arrived(sx.at[:, other, :], xsem.at[1])

    def targets_out(sends):
        for t in range(4):
            v = tgt[t].astype(F32)
            tg_send[t] = half_of(v, o)
            tg[t, own, :] = half_of(v, c)
        rcopy(tg_send, tg.at[:, own, :], xsem.at[2], xsem.at[3], sib, sends)

    def codes():
        for s in range(2):
            TK[s] = jnp.transpose(jnp.broadcast_to(tok[s : s + 1, :].astype(F32), (128, 384)))
        FC[...] = fc[...].astype(F32)

    yp, y2, ym = ys
    lo, hi = pl.ds(0, MID), pl.ds(MID, MID)
    count = [0]

    def gsend(src_ref, at, cols, to, rsem, sends):
        dst = X.at[at] if cols is None else X.at[at + (slice(None), cols)]
        a = src_ref if cols is None else src_ref.at[:, cols]
        rcopy(a, dst, ags.at[count[0]], rsem, to, sends)
        count[0] += 1

    def rsem_of(g, ll, yy, part=0):
        return agr.at[g, ll, yy, part]

    def both(g, ll, yy, sends):
        at = (c, g, ll, yy)
        gsend(X.at[at], at, None, sib, br.at[g, ll, yy], sends)

    def gather_first(g, sends):
        at = (c, g, l, y)
        r = X.at[at]
        for to in (yp, ym):
            gsend(r, at, None, dev(y=to), rsem_of(g, l, y), sends)
        if g == 0:
            gsend(XO.at[g], at, None, zo, rsem_of(g, l, y), sends)
        elif g == 1:
            gsend(r, at, None, zp, rsem_of(g, l, y), sends)
        else:
            gsend(XO.at[g], at, lo, zo, rsem_of(g, l, y, 0), sends)
            gsend(r, at, hi, zp, rsem_of(g, l, y, 1), sends)
        both(g, l, y, sends)

    def wait_z(g):
        if g < 2:
            arrived(X.at[c, g, 1 - l, y], rsem_of(g, 1 - l, y))
        else:
            arrived(X.at[c, g, 1 - l, y, :, lo], rsem_of(g, 1 - l, y, 0))
            arrived(X.at[c, g, 1 - l, y, :, hi], rsem_of(g, 1 - l, y, 1))

    def gather_own(sends):
        for g in range(GRP):
            for frm, to, cols, part in ((ym, yp, lo, 0), (yp, ym, hi, 1)):
                at = (c, g, l, frm)
                arrived(X.at[at], rsem_of(g, l, frm))
                gsend(X.at[at], at, cols, dev(y=to), rsem_of(g, l, frm, part), sends)
                both(g, l, frm, sends)
        for g in range(GRP):
            at = (c, g, 1 - l, y)
            wait_z(g)
            for to in (yp, ym, y2):
                gsend(X.at[at], at, None, dev(y=to), rsem_of(g, 1 - l, y), sends)
            both(g, 1 - l, y, sends)
        for g in range(GRP):
            arrived(X.at[c, g, l, y2, :, lo], rsem_of(g, l, y2, 0))
            arrived(X.at[c, g, l, y2, :, hi], rsem_of(g, l, y2, 1))
            both(g, l, y2, sends)
        for g in range(GRP):
            for yy in range(4):
                arrived(X.at[o, g, l, yy], br.at[g, l, yy])

    def gather_rest(sends):
        for g in range(GRP):
            for frm in (ym, yp, y2):
                arrived(X.at[c, g, 1 - l, frm], rsem_of(g, 1 - l, frm))
                both(g, 1 - l, frm, sends)
        for g in range(GRP):
            for yy in range(4):
                arrived(X.at[o, g, 1 - l, yy], br.at[g, 1 - l, yy])

    def errors_first(g, sends):
        at = (c, g, l, y)
        r = X.at[at]
        gsend(XO.at[g], at, None, zo, rsem_of(g, l, y), sends)
        for to in (yp, ym):
            gsend(r, at, None, dev(y=to), rsem_of(g, l, y), sends)
        both(g, l, y, sends)

    def from_y(g, ll, sends, on_z):
        for frm, to, cols, part in ((ym, yp, lo, 0), (yp, ym, hi, 1)):
            at = (c, g, ll, frm)
            arrived(X.at[at], rsem_of(g, ll, frm))
            gsend(X.at[at], at, cols, dev(y=to), rsem_of(g, ll, frm, part), sends)
            if on_z:
                gsend(X.at[at], at, None, zp, rsem_of(g, ll, frm), sends)
            both(g, ll, frm, sends)

    def from_y2(g, ll, sends, on_z):
        at = (c, g, ll, y2)
        arrived(X.at[at + (slice(None), lo)], rsem_of(g, ll, y2, 0))
        arrived(X.at[at + (slice(None), hi)], rsem_of(g, ll, y2, 1))
        if on_z:
            gsend(X.at[at], at, None, zp, rsem_of(g, ll, y2), sends)
        both(g, ll, y2, sends)

    def from_z(g, yy, sends, on_y):
        at = (c, g, 1 - l, yy)
        arrived(X.at[at], rsem_of(g, 1 - l, yy))
        if on_y:
            for to in (yp, ym):
                gsend(X.at[at], at, None, dev(y=to), rsem_of(g, 1 - l, yy), sends)
        both(g, 1 - l, yy, sends)

    def gather_errors(sends):
        from_z(0, y, sends, True)
        from_y(0, l, sends, False)
        from_y(1, l, sends, True)
        from_y(2, l, sends, True)
        from_y(0, 1 - l, sends, False)
        from_y2(1, l, sends, True)
        from_y2(2, l, sends, True)
        from_y2(0, l, sends, False)
        from_z(1, y, sends, False)
        from_z(2, y, sends, False)
        for g in (1, 2):
            for yy in (ym, yp):
                from_z(g, yy, sends, False)
        from_y2(0, 1 - l, sends, False)
        for g in (1, 2):
            from_z(g, y2, sends, False)
        for g in range(GRP):
            for ll in range(2):
                for yy in range(4):
                    arrived(X.at[o, g, ll, yy], br.at[g, ll, yy])

    def against(lh, rows):
        total = None
        for cc in range(2):
            for g in range(GRP):
                a = X[cc, g].reshape(384, GW) if lh is None else X[cc, g, lh].reshape(192, GW)
                b = W[rows, cc * HALF + g * GW : cc * HALF + (g + 1) * GW]
                d = lax.dot_general(a, b, NT, preferred_element_type=F32)
                total = d if total is None else total + d
        return total

    def piece(s, i):
        return s, lax.rem(l + i // NCH, 2), lax.rem(i, NCH)

    def fcopy(s, i, way, to, sem=None):
        s, lh, k = piece(s, i)
        r = FB.at[s, lh, k, way]
        return copy(r, r, (fs if sem is None else sem).at[s, lh, k, way], fr.at[s, lh, k, way], to)

    def farrived(s, i, way):
        s, lh, k = piece(s, i)
        arrived(FB.at[s, lh, k, way], fr.at[s, lh, k, way])

    def crosses0(i):
        return lax.rem(i, NCH) < CROSS0

    def encode():
        sends = []
        sources_in(sends)
        for g in range(GRP):
            cols = slice(GW * g, GW * (g + 1))
            X[c, g, l, y] = sx[h, :, cols].astype(BF16)
            XO[g] = sx[1 - h, :, cols].astype(BF16)
            gather_first(g, sends)
        targets_out(sends)
        codes()
        gather_own(sends)
        line = (dev(x=1), dev(x=3))

        def chunk(i, _):
            _, lh, k = piece(h, i)
            rows = pl.ds(pl.multiple_of(k * CH, CH), CH)

            @pl.when(i < NCH)
            def _():
                pltpu.make_async_copy(w_hbm.at[0, rows], W.at[rows], wsem.at[k]).wait()

            pre = against(lh, rows) + bias[pl.ds(h, 1), rows]
            toks = TK[h, pl.ds(pl.multiple_of(lh * 192, 8), 192), :]
            on = gate_of(jnp.concatenate([toks] * 2, axis=1), FC[pl.ds(h, 1), rows])
            FB[h, lh, k] = jnp.where(on, pre, 0.0).astype(BF16).reshape(2, SUB, CH)
            for way in range(2):
                fcopy(h, i, way, line[way]).start()

            @pl.when(crosses0(i))
            def _():
                for way in range(2):
                    fcopy(h, i, way, cross, fcs).start()

            j = i - FLAG

            @pl.when((j >= 0) & crosses0(j + NCH))
            def _():
                for way in range(2):
                    farrived(1 - h, j, way)
                    fcopy(1 - h, j, way, line[way]).start()

            return 0

        lax.fori_loop(0, NCH, chunk, 0)
        gather_rest(sends)
        lax.fori_loop(NCH, STEPS, chunk, 0)

        def drain(i, _):
            for way in range(2):
                fcopy(h, i, way, line[way]).wait_send()

                @pl.when(crosses0(i))
                def _():
                    fcopy(h, i, way, cross, fcs).wait_send()
                    fcopy(1 - h, i, way, line[way]).wait_send()

            return 0

        lax.fori_loop(0, STEPS, drain, 0)
        for cp in sends:
            cp.wait_send()
        arrived(tg.at[:, other, :], xsem.at[3])

    def lh_of(j):
        return l if j == 0 else 1 - l

    def fold_start(j, sends):
        for g in range(GRP):
            cols = slice(GW * g, GW * (g + 1))
            S[j, g] = acc[o, lh_of(j), :, cols].astype(BF16).reshape(4, ROWS, GW)
            rcopy(S.at[j, g], C.at[j, g], ss.at[j, g], sr.at[j, g], sib, sends)

    def fold_end(j, sends):
        for g in range(GRP):
            cols = slice(GW * g, GW * (g + 1))
            arrived(C.at[j, g], sr.at[j, g])
            v = acc[c, lh_of(j), :, cols] + C[j, g].astype(F32).reshape(192, GW)
            T[j, g] = v.astype(BF16).reshape(4, ROWS, GW)
            for k in (0, 2, 1):
                rcopy(T.at[j, g, ys[k]], RY.at[j, g, 2 - k], ys_s.at[j, g, k], ys_r.at[j, g, 2 - k], dev(y=ys[k]), sends)

    def fold_sum(j, g):
        for k in range(3):
            arrived(RY.at[j, g, k], ys_r.at[j, g, k])
        v = T[j, g, y].astype(F32)
        for k in range(3):
            v = v + RY[j, g, k].astype(F32)
        return v

    def decode():
        sends = []
        acc[...] = jnp.zeros_like(acc)
        xin = []
        sources_in(xin)
        targets_out(xin)
        codes()
        nxt = (dev(x=lax.rem(x + 1, 4)), dev(x=lax.rem(x + 3, 4)))
        more = (x < 3, x > 1)
        lag = ((x - 1) * LH, (3 - x) * LH)
        mine_src = (dm[layer - 2] >= 3).astype(jnp.int32)

        def step(t, _):
            for way in range(2):
                i = t - lag[way]

                @pl.when((i >= 0) & (i < STEPS))
                def _():
                    farrived(h, i, way)

                    @pl.when(more[way])
                    def _():
                        fcopy(h, i, way, nxt[way]).start()

                    @pl.when(jnp.logical_not(crosses0(i)))
                    def _():
                        fcopy(h, i, way, cross, fcs).start()

                j = i - FLAG

                @pl.when((j >= 0) & (j < STEPS) & crosses0(j + 2 * NCH))
                def _():
                    farrived(1 - h, j, way)

                    @pl.when(more[way])
                    def _():
                        fcopy(1 - h, j, way, nxt[way]).start()

            m = t - ML

            @pl.when(m >= 0)
            def _():
                @pl.when(jnp.logical_not(crosses0(m)))
                def _():
                    for way in range(2):
                        farrived(1 - h, m, way)

                _, lh, k = piece(h, m)
                rows = pl.ds(pl.multiple_of(k * CH, CH), CH)

                @pl.when(m < NCH)
                def _():
                    pltpu.make_async_copy(w_hbm.at[0, rows], W.at[rows], wsem.at[k]).wait()

                a = jnp.where(mine_src == 0, FB[0, lh, k], FB[1, lh, k]).reshape(192, CH)
                for cc in range(2):
                    for n in range(GRP):
                        cols = slice(cc * HALF + n * GW, cc * HALF + (n + 1) * GW)
                        acc[cc, lh, :, n * GW : (n + 1) * GW] += jnp.dot(a, W[rows, cols], preferred_element_type=F32)

            return 0

        lax.fori_loop(0, NCH + ML, step, 0)
        fold_start(0, sends)
        lax.fori_loop(NCH + ML, NCH + ML + 2, step, 0)
        fold_end(0, sends)
        lax.fori_loop(NCH + ML + 2, STEPS + ML, step, 0)
        fold_start(1, sends)
        fold_end(1, sends)

        def drain(i, _):
            for way in range(2):

                @pl.when(more[way])
                def _():
                    fcopy(h, i, way, nxt[way]).wait_send()

                    @pl.when(crosses0(i))
                    def _():
                        fcopy(1 - h, i, way, nxt[way]).wait_send()

                @pl.when(jnp.logical_not(crosses0(i)))
                def _():
                    fcopy(h, i, way, cross, fcs).wait_send()

            return 0

        lax.fori_loop(0, STEPS, drain, 0)
        for cp in xin:
            cp.wait_send()
        arrived(tg.at[:, other, :], xsem.at[3])
        for g in range(GRP + 1):
            if g < GRP:
                V1[g] = fold_sum(1, g).astype(BF16)
                rcopy(V1.at[g], RZ.at[g], zs.at[g], zr.at[g], zp, sends)
            if g > 0:
                v = fold_sum(0, g - 1)
                arrived(RZ.at[g - 1], zr.at[g - 1])
                RL[g - 1][layer] = (v + RZ[g - 1].astype(F32)).astype(BF16)
                lcopy(g - 1, layer, 0, cross).start()
                for k in range(3):
                    lcopy(g - 1, layer, 1 + k, dev(x=xs[k])).start()
        for cp in sends:
            cp.wait_send()

    def lcopy(g, m, n, to):
        r = RL[g].at[m]
        return copy(r, r, ls.at[g, n], lr.at[g, m], to)

    def lwait(g, m):
        arrived(RL[g].at[m], lr.at[g, m])

    def exchange(g):
        pair = 2 * x + 1 - h
        if g == ZG:

            @pl.when(x > 0)
            def _():
                lwait(g, pair)
                for k in range(3):
                    lcopy(g, pair, 4 + k, dev(x=xs[k])).start()

        else:
            for k in (0, 2, 1):

                @pl.when(xs[k] > 0)
                def _():
                    m = 2 * xs[k] + h
                    lwait(g, m)
                    lcopy(g, m, 4 + k, cross).start()

    def exchanged(g):
        for k in range(3):

            @pl.when(xs[k] > 0)
            def _():
                lwait(g, 2 * xs[k] + 1 - h)
                if g == ZG:
                    lwait(g, 2 * xs[k] + h)

        if g != ZG:

            @pl.when(x > 0)
            def _():
                lwait(g, 2 * x + 1 - h)

    def exchange_drain():
        @pl.when(x > 0)
        def _():
            for g in range(GRP):
                lcopy(g, layer, 0, cross).wait_send()
                for k in range(3):
                    lcopy(g, layer, 1 + k, dev(x=xs[k])).wait_send()
            for k in range(3):
                lcopy(ZG, 2 * x + 1 - h, 4 + k, dev(x=xs[k])).wait_send()

        for g in range(GRP):
            if g == ZG:
                continue
            for k in range(3):

                @pl.when(xs[k] > 0)
                def _():
                    lcopy(g, 2 * xs[k] + h, 4 + k, cross).wait_send()

    place = []
    for p in range(6):
        at = jnp.int32(2)
        for i in range(6):
            at = jnp.where(dm[i] == p, jnp.int32(i + 2), at)
        place.append(at)

    def target_of(m):
        pair = dm[jnp.maximum(m - 2, 0)]
        return jnp.where(pair >= 3, pair - 2, pair)

    def recon(g, sends):
        for t in range(4):
            v = RL[g][place[PAIRS[t][0]]].astype(F32)
            for q in PAIRS[t][1:]:
                v = v + RL[g][place[q]].astype(F32)
            E[g, t] = v
        rcopy(E.at[g, :, other, :], ER.at[g], es.at[g], er.at[g], sib, sends)

    def recon_out():
        for g in range(GRP):
            arrived(ER.at[g], er.at[g])
            for cc in range(2):
                cols = slice(cc * HALF + GW * g, cc * HALF + GW * (g + 1))
                rec_out[:, :, cols] = jnp.where(c == cc, E[g, :, own, :], ER[g])

    def gcopy(n, k):
        to = xs[k]
        return copy(GS.at[n, pl.ds(2 * to, 2)], GA.at[n, x], gs.at[n, k], gr.at[n, x], dev(x=to))

    def zcopy(n):
        return copy(GC_.at[n], GZ.at[n], gzs.at[n], gzr.at[n], cross)

    def line_sum(n):
        for k in range(3):

            @pl.when(xs[k] > 0)
            def _():
                arrived(GA.at[n, xs[k]], gr.at[n, xs[k]])

        for s in range(2):
            mine, far = None, None
            for a in range(1, 4):
                on = (dm[2 * a + h - 2] >= 3) == (s == 1)
                p = jnp.where(on, GA[n, a, h].astype(F32), 0.0)
                q = jnp.where(on, GA[n, a, 1 - h].astype(F32), 0.0)
                mine = p if mine is None else mine + p
                far = q if far is None else far + q
            GO[n, s] = mine
            GC_[n, s] = far.astype(BF16)
        zcopy(n).start()

    def grads():
        def chunk(n, _):
            rows = pl.ds(pl.multiple_of(n * GC, GC), GC)
            GS[n] = against(None, rows).astype(BF16).reshape(8, ROWS, GC)
            for k in (0, 2, 1):
                gcopy(n, k).start()
            GA[n, x] = GS[n, pl.ds(2 * x, 2)]

            @pl.when(n >= GLAG)
            def _():
                line_sum(n - GLAG)

            return 0

        lax.fori_loop(0, GN, chunk, 0)

    def line_sums(start):
        def one(n, _):
            line_sum(n)
            return 0

        lax.fori_loop(start, GN, one, 0)

    def grads_drain():
        def drain(n, _):
            for k in range(3):
                gcopy(n, k).wait_send()
            return 0

        lax.fori_loop(0, GN, drain, 0)

    def grads_out():
        rows = pl.ds(pl.multiple_of(ROWS * layer, 8), ROWS)
        for n in range(GN):
            cols = slice(GC * n, GC * (n + 1))
            arrived(GZ.at[n], gzr.at[n])
            for s in range(2):
                v = GO[n, s] + GZ[n, s].astype(F32)
                on = gate_of(jnp.concatenate([TK[s, rows, :]] * (GC // 128), axis=1), FC[s : s + 1, cols])
                pg_out[s, :, cols] = jnp.where(on, v, 0.0).astype(BF16)
        for n in range(GN):
            zcopy(n).wait_send()

    def error_block(g, sends):
        cols = slice(GW * g, GW * (g + 1))
        for dst, t in ((X.at[c, g, l, y], target_of(layer)), (XO.at[g], target_of(2 * x + 1 - h))):
            dst[...] = (E[g, t] - tg[t, :, cols]).astype(BF16)
        errors_first(g, sends)

    def decoder_rest():
        sends = []
        count[0] = 0
        for g in range(GRP):
            exchange(g)
        for g in range(GRP):
            exchanged(g)
            recon(g, sends)
            error_block(g, sends)
        gather_errors(sends)
        grads()
        recon_out()
        line_sums(GN - GLAG)
        for cp in sends:
            cp.wait_send()
        grads_drain()

    def encoder_rest():
        sends = []
        for g in range(GRP):
            exchange(g)
        for g in range(GRP):
            exchanged(g)
            recon(g, sends)
        recon_out()
        line_sums(0)
        for cp in sends:
            cp.wait_send()

    enter()
    pl.when(x == 0)(encode)
    pl.when(x > 0)(decode)
    pl.when(x > 0)(decoder_rest)
    pl.when(x == 0)(encoder_rest)
    grads_out()
    exchange_drain()


def body(sources, targets, blocks, enc_bias, token_code, feature_threshold_code, dec_map):
    vm = pl.BlockSpec(memory_space=pltpu.VMEM)
    V = pltpu.VMEM
    D = pltpu.SemaphoreType.DMA
    recon, pre_grads = pl.pallas_call(
        kernel,
        out_shape=(
            jax.ShapeDtypeStruct((4, 24, 4608), F32),
            jax.ShapeDtypeStruct((2, 48, 2048), BF16),
        ),
        in_specs=[pl.BlockSpec(memory_space=pltpu.SMEM), vm, vm, pl.BlockSpec(memory_space=pl.ANY), vm, vm, vm],
        out_specs=(vm, vm),
        scratch_shapes=[
            V((2048, 4608), BF16),
            V((2, GRP, 2, 4, ROWS, GW), BF16),
            V((GRP, ROWS, GW), BF16),
            V((2, 2, NCH, 2, SUB, CH), BF16),
            V((2, 2, 192, HALF), F32),
            V((2, 24, HALF), F32),
            V((2, ROWS, HALF), F32),
            V((4, 24, HALF), F32),
            V((4, ROWS, HALF), F32),
            V((2, 384, 128), F32),
            V((2, 2048), F32),
            V((2, GRP, 4, ROWS, GW), BF16),
            V((2, GRP, 4, ROWS, GW), BF16),
            V((2, GRP, 4, ROWS, GW), BF16),
            V((2, GRP, 3, ROWS, GW), BF16),
            V((GRP, ROWS, GW), BF16),
            V((GRP, ROWS, GW), BF16),
            V((8, ROWS, GW), BF16),
            V((8, ROWS, GW), BF16),
            V((8, ROWS, GW), BF16),
            V((GRP, 4, ROWS, GW), F32),
            V((GRP, 4, 24, GW), F32),
            V((GN, 8, ROWS, GC), BF16),
            V((GN, 4, 2, ROWS, GC), BF16),
            V((GN, 2, ROWS, GC), F32),
            V((GN, 2, ROWS, GC), BF16),
            V((GN, 2, ROWS, GC), BF16),
            D((NCH,)),
            D((4,)),
            D((64,)),
            D((GRP, 2, 4, 2)),
            D((GRP, 2, 4)),
            D((2, 2, NCH, 2)),
            D((2, 2, NCH, 2)),
            D((2, 2, NCH, 2)),
            D((2, GRP)),
            D((2, GRP)),
            D((2, GRP, 3)),
            D((2, GRP, 3)),
            D((GRP,)),
            D((GRP,)),
            D((GRP, 7)),
            D((GRP, 8)),
            D((GRP,)),
            D((GRP,)),
            D((GN, 3)),
            D((GN, 4)),
            D((GN,)),
            D((GN,)),
        ],
        compiler_params=pltpu.CompilerParams(
            collective_id=1, has_side_effects=True, vmem_limit_bytes=62 * 2**20
        ),
        name="transcoder",
    )(dec_map, sources, targets, blocks, enc_bias, token_code, feature_threshold_code)
    return recon - targets.astype(F32), pre_grads


def solution(mesh):
    return jax.shard_map(
        body,
        mesh=mesh,
        in_specs=(
            P(None, "feat", None),
            P(None, "feat", None),
            P("layer", "feat", None),
            P(None, "feat"),
            P(),
            P(None, "feat"),
            P(),
        ),
        out_specs=(P(None, "feat", None), P(None, "layer", "feat")),
        check_vma=False,
    )
```

time: 599 us -> 142 us (0.24)
  waiting for transfers between devices: 539 us -> 0 us
  Pallas kernels: 0 us -> 137 us
  between operations: 16.2 us -> 0.67 us
  matrix products: 13.5 us -> 0 us
  other arithmetic: 15.9 us -> 2.9 us
  local copies, waits for them, and re-layouts: 10.2 us -> 0.75 us
    psum x3 -> x0, waiting for transfers between devices: 384 us -> none  [the longest x1 156 us: body(): total = lax.psum(terms.astype(jnp.bfloat16), 'layer').astype(jnp.float32)]
    pallas_call x0 -> x1, Pallas kernels: none -> 137 us  [body(): pl.pallas_call(kernel, out_shape=(jax.ShapeDtypeStruct((4, 24, 4608), F32...]
    all_gather x2 -> x0, waiting for transfers between devices: 79 us -> none  [the longest x1 39.6 us: body(): against_piece = lax.all_gather(error_low, 'feat', axis=0, tiled=True)]
    reduce_scatter x1 -> x0, waiting for transfers between devices: 76.3 us -> none  [body(): lax.psum_scatter(lax.cond(encoder, lambda: jnp.zeros((count, weight.shape...]
    dot_general x1 -> x0, matrix products: 13.5 us -> none  [body(): lax.dot_general(piece, weight, contract_last, preferred_element_type=jnp....]
    convert_element_type x4 -> x0, other arithmetic: 8.62 us -> none  [the longest x1 4.27 us: body(): total = lax.psum(terms.astype(jnp.bfloat16), 'layer').astype(jnp.float32)]
  transfers between devices with their start and end apart: 6 -> 0, of which waited for: 6 -> 0; matrix products, arithmetic and copies ran while one was open for 1% -> 0% of each run, Pallas kernels for 0% -> 0%
where the time goes in v2:
time: 142 us; the launch traced here: 141 us
  Pallas kernels  137 us (96%)
  other arithmetic  2.9 us (2%)
    pallas_call x1, Pallas kernels, body(): pl.pallas_call(kernel, out_shape=(jax.ShapeDtypeStruct((4, 24, 4608), F32...  137 us
    sub x1, other arithmetic, body(): return (recon - targets.astype(F32), pre_grads)  2.9 us

profile of v2, /device:TPU:1, one launch (start us, length us, event | category | flops | bytes accessed | tf_op | source)
XLA Modules:
  0.0 141.4 jit_solution(16901643649325151986)
XLA Ops:
  0.6 0.0 copy-start
  0.6 137.1 %transcoder.1 = (f32[4,24,4608]{2,1,0:T(8,128)}, bf16[2,48,2048]{2,1,0:T(8,128)(2,1)}) custom-call(s32[6]{0:T(128)} %dm.1, bf16[2,24,4608]{2,1,0:T(8,128)(2,1)} %src.1, bf16[4,24,4608]{2,1,0:T(8,128)(2,1)} %tgt.1, bf16[1,2048,4608]{2,1,0:T(8,128)(2,1)} %w_hbm.1, f32[2,2048]{1,0:T(2,128)} %bias.1, s32[2,384]{1,0:T(2,128)} %tok.1, s32[2,2048]{1,0:T(2,128)} %fc.1), custom_call_target="tpu_custom_call" | custom-call | tf_op jit(solution)/shard_map/transcoder/pallas_call | solution.py:657
  137.7 0.0 copy-done
  137.8 0.0 copy-start.1
  137.8 2.9 %convert_subtract_fusion = f32[4,24,4608]{2,1,0:T(8,128)} fusion(f32[4,24,4608]{2,1,0:T(8,128)} %get-tuple-element.4, bf16[4,24,4608]{2,1,0:T(8,128)(2,1)S(1)} %copy-done), kind=kLoop, calls=%fused_computation | loop fusion | flops 884736 | bytes 4423680 | tf_op jit(solution)/shard_map/sub | solution.py:721
  140.7 0.0 copy-done.1
  140.7 0.7 copy.10
Async XLA Ops:
  0.6 137.1 %copy-start = (bf16[4,24,4608]{2,1,0:T(8,128)(2,1)S(1)}, bf16[4,24,4608]{2,1,0:T(8,128)(2,1)}, u32[]{:S(2)}) copy-start(bf16[4,24,4608]{2,1,0:T(8,128)(2,1)} %tgt.1) | copy-start | bytes 2654212
  137.8 2.9 %copy-start.1 = (bf16[2,48,2048]{2,1,0:T(8,128)(2,1)S(1)}, bf16[2,48,2048]{2,1,0:T(8,128)(2,1)}, u32[]{:S(2)}) copy-start(bf16[2,48,2048]{2,1,0:T(8,128)(2,1)} %get-tuple-element.9) | copy-start | bytes 1179652

commit v3 on v2

--- a/solution.py
+++ b/solution.py
@@ -11,9 +11,9 @@
 
 ROWS = 48
 HALF = 2304
-GRP = 3
-GW = 768
-MID = 384
+GRP = 6
+GW = 384
+DW = 768
 NCH = 8
 CH = 256
 SUB = 96
@@ -25,7 +25,11 @@
 GN = 8
 GC = 256
 GLAG = 3
-ZG = 2
+ZG = (3, 4, 5)
+LC = 2
+LX = 5
+LE = 9
+GL = 3
 
 NT = (((1,), (1,)), ((), ()))
 PAIRS = ((0,), (1, 3), (2, 4), (5,))
@@ -40,15 +44,15 @@
 def kernel(
     dm, src, tgt, w_hbm, bias, tok, fc, rec_out, pg_out,
     W, X, XO, FB, acc, sx_send, sx, tg_send, tg, TK, FC,
-    S, C, T, RY, V1, RZ, R0, R1, R2, E, ER, GS, GA, GO, GC_, GZ,
-    wsem, xsem, ags, agr, br, fs, fcs, fr, ss, sr, ys_s, ys_r, zs, zr, ls, lr, es, er, gs, gr, gzs, gzr,
+    S, C, T, RY, V1, RZ, R0, R1, R2, R3, R4, R5, E, ER, RO, GS, GA, GO, GC_, GZ,
+    wsem, xsem, ags, agr, br, fs, fcs, fr, ss, sr, ys_s, ys_r, zs, zr, ls, lr, es, er, gs, gr, gzs, gzr, osem,
 ):
     layer = lax.axis_index("layer")
     feat = lax.axis_index("feat")
     x, h = layer // 2, layer % 2
     l, y, c = feat // 8, (feat // 2) % 4, feat % 2
     o = 1 - c
-    RL = (R0, R1, R2)
+    RL = (R0, R1, R2, R3, R4, R5)
 
     def dev(x=x, h=h, l=l, y=y, c=c):
         return (2 * x + h, (4 * l + y) * 2 + c)
@@ -110,7 +114,11 @@
         FC[...] = fc[...].astype(F32)
 
     yp, y2, ym = ys
-    lo, hi = pl.ds(0, MID), pl.ds(MID, MID)
+
+    def parts(g):
+        m = 128 if g % 2 == 0 else 256
+        return pl.ds(0, m), pl.ds(m, GW - m)
+
     count = [0]
 
     def gsend(src_ref, at, cols, to, rsem, sends):
@@ -131,24 +139,15 @@
         r = X.at[at]
         for to in (yp, ym):
             gsend(r, at, None, dev(y=to), rsem_of(g, l, y), sends)
-        if g == 0:
+        if g % 2 == 0:
             gsend(XO.at[g], at, None, zo, rsem_of(g, l, y), sends)
-        elif g == 1:
+        else:
             gsend(r, at, None, zp, rsem_of(g, l, y), sends)
-        else:
-            gsend(XO.at[g], at, lo, zo, rsem_of(g, l, y, 0), sends)
-            gsend(r, at, hi, zp, rsem_of(g, l, y, 1), sends)
         both(g, l, y, sends)
 
-    def wait_z(g):
-        if g < 2:
-            arrived(X.at[c, g, 1 - l, y], rsem_of(g, 1 - l, y))
-        else:
-            arrived(X.at[c, g, 1 - l, y, :, lo], rsem_of(g, 1 - l, y, 0))
-            arrived(X.at[c, g, 1 - l, y, :, hi], rsem_of(g, 1 - l, y, 1))
-
     def gather_own(sends):
         for g in range(GRP):
+            lo, hi = parts(g)
             for frm, to, cols, part in ((ym, yp, lo, 0), (yp, ym, hi, 1)):
                 at = (c, g, l, frm)
                 arrived(X.at[at], rsem_of(g, l, frm))
@@ -156,11 +155,12 @@
                 both(g, l, frm, sends)
         for g in range(GRP):
             at = (c, g, 1 - l, y)
-            wait_z(g)
+            arrived(X.at[at], rsem_of(g, 1 - l, y))
             for to in (yp, ym, y2):
                 gsend(X.at[at], at, None, dev(y=to), rsem_of(g, 1 - l, y), sends)
             both(g, 1 - l, y, sends)
         for g in range(GRP):
+            lo, hi = parts(g)
             arrived(X.at[c, g, l, y2, :, lo], rsem_of(g, l, y2, 0))
             arrived(X.at[c, g, l, y2, :, hi], rsem_of(g, l, y2, 1))
             both(g, l, y2, sends)
@@ -186,6 +186,7 @@
         both(g, l, y, sends)
 
     def from_y(g, ll, sends, on_z):
+        lo, hi = parts(g)
         for frm, to, cols, part in ((ym, yp, lo, 0), (yp, ym, hi, 1)):
             at = (c, g, ll, frm)
             arrived(X.at[at], rsem_of(g, ll, frm))
@@ -195,6 +196,7 @@
             both(g, ll, frm, sends)
 
     def from_y2(g, ll, sends, on_z):
+        lo, hi = parts(g)
         at = (c, g, ll, y2)
         arrived(X.at[at + (slice(None), lo)], rsem_of(g, ll, y2, 0))
         arrived(X.at[at + (slice(None), hi)], rsem_of(g, ll, y2, 1))
@@ -210,23 +212,28 @@
                 gsend(X.at[at], at, None, dev(y=to), rsem_of(g, 1 - l, yy), sends)
         both(g, 1 - l, yy, sends)
 
-    def gather_errors(sends):
-        from_z(0, y, sends, True)
-        from_y(0, l, sends, False)
-        from_y(1, l, sends, True)
-        from_y(2, l, sends, True)
-        from_y(0, 1 - l, sends, False)
-        from_y2(1, l, sends, True)
-        from_y2(2, l, sends, True)
-        from_y2(0, l, sends, False)
-        from_z(1, y, sends, False)
-        from_z(2, y, sends, False)
-        for g in (1, 2):
-            for yy in (ym, yp):
-                from_z(g, yy, sends, False)
-        from_y2(0, 1 - l, sends, False)
-        for g in (1, 2):
+    def gather_errors(g, n, sends):
+        if g in ZG:
+            if n == 0:
+                from_z(g, y, sends, True)
+                from_y(g, l, sends, False)
+            elif n == 1:
+                from_y(g, 1 - l, sends, False)
+                from_y2(g, l, sends, False)
+            elif n == 2:
+                from_y2(g, 1 - l, sends, False)
+        elif n == 0:
+            from_y(g, l, sends, True)
+        elif n == 1:
+            from_y2(g, l, sends, True)
+            from_z(g, y, sends, False)
+        elif n == 2:
+            from_z(g, ym, sends, False)
+            from_z(g, yp, sends, False)
+        else:
             from_z(g, y2, sends, False)
+
+    def gathered():
         for g in range(GRP):
             for ll in range(2):
                 for yy in range(4):
@@ -235,9 +242,10 @@
     def against(lh, rows):
         total = None
         for cc in range(2):
-            for g in range(GRP):
-                a = X[cc, g].reshape(384, GW) if lh is None else X[cc, g, lh].reshape(192, GW)
-                b = W[rows, cc * HALF + g * GW : cc * HALF + (g + 1) * GW]
+            for n in range(HALF // DW):
+                a = [X[cc, g] if lh is None else X[cc, g, lh] for g in (2 * n, 2 * n + 1)]
+                a = jnp.concatenate([v.reshape(-1, GW) for v in a], axis=1)
+                b = W[rows, cc * HALF + n * DW : cc * HALF + (n + 1) * DW]
                 d = lax.dot_general(a, b, NT, preferred_element_type=F32)
                 total = d if total is None else total + d
         return total
@@ -402,9 +410,9 @@
 
                 a = jnp.where(mine_src == 0, FB[0, lh, k], FB[1, lh, k]).reshape(192, CH)
                 for cc in range(2):
-                    for n in range(GRP):
-                        cols = slice(cc * HALF + n * GW, cc * HALF + (n + 1) * GW)
-                        acc[cc, lh, :, n * GW : (n + 1) * GW] += jnp.dot(a, W[rows, cols], preferred_element_type=F32)
+                    for n in range(HALF // DW):
+                        cols = slice(cc * HALF + n * DW, cc * HALF + (n + 1) * DW)
+                        acc[cc, lh, :, n * DW : (n + 1) * DW] += jnp.dot(a, W[rows, cols], preferred_element_type=F32)
 
             return 0
 
@@ -416,6 +424,38 @@
         fold_start(1, sends)
         fold_end(1, sends)
 
+        arrived(tg.at[:, other, :], xsem.at[3])
+        count[0] = 0
+        for t in range(GRP + LE + 4 * GL):
+            g = t
+            if g < GRP:
+                V1[g] = fold_sum(1, g).astype(BF16)
+                rcopy(V1.at[g], RZ.at[g], zs.at[g], zr.at[g], zp, sends)
+            g = t - LC
+            if 0 <= g < GRP:
+                v = fold_sum(0, g)
+                arrived(RZ.at[g], zr.at[g])
+                RL[g][layer] = (v + RZ[g].astype(F32)).astype(BF16)
+                lcopy(g, layer, 0, cross).start()
+                for k in range(3):
+                    lcopy(g, layer, 1 + k, dev(x=xs[k])).start()
+            g = t - LX
+            if 0 <= g < GRP:
+                exchange(g)
+            g = t - LE
+            if 0 <= g < GRP:
+                exchanged(g)
+                recon(g, sends)
+                error_block(g, sends)
+            for n in range(4):
+                g = t - LE - GL * (n + 1)
+                if 0 <= g < GRP:
+                    gather_errors(g, n, sends)
+        gathered()
+        grads()
+        recon_out()
+        line_sums(GN - GLAG)
+
         def drain(i, _):
             for way in range(2):
 
@@ -436,20 +476,9 @@
         lax.fori_loop(0, STEPS, drain, 0)
         for cp in xin:
             cp.wait_send()
-        arrived(tg.at[:, other, :], xsem.at[3])
-        for g in range(GRP + 1):
-            if g < GRP:
-                V1[g] = fold_sum(1, g).astype(BF16)
-                rcopy(V1.at[g], RZ.at[g], zs.at[g], zr.at[g], zp, sends)
-            if g > 0:
-                v = fold_sum(0, g - 1)
-                arrived(RZ.at[g - 1], zr.at[g - 1])
-                RL[g - 1][layer] = (v + RZ[g - 1].astype(F32)).astype(BF16)
-                lcopy(g - 1, layer, 0, cross).start()
-                for k in range(3):
-                    lcopy(g - 1, layer, 1 + k, dev(x=xs[k])).start()
         for cp in sends:
             cp.wait_send()
+        grads_drain()
 
     def lcopy(g, m, n, to):
         r = RL[g].at[m]
@@ -460,7 +489,7 @@
 
     def exchange(g):
         pair = 2 * x + 1 - h
-        if g == ZG:
+        if g in ZG:
 
             @pl.when(x > 0)
             def _():
@@ -483,10 +512,10 @@
             @pl.when(xs[k] > 0)
             def _():
                 lwait(g, 2 * xs[k] + 1 - h)
-                if g == ZG:
+                if g in ZG:
                     lwait(g, 2 * xs[k] + h)
 
-        if g != ZG:
+        if g not in ZG:
 
             @pl.when(x > 0)
             def _():
@@ -499,11 +528,12 @@
                 lcopy(g, layer, 0, cross).wait_send()
                 for k in range(3):
                     lcopy(g, layer, 1 + k, dev(x=xs[k])).wait_send()
-            for k in range(3):
-                lcopy(ZG, 2 * x + 1 - h, 4 + k, dev(x=xs[k])).wait_send()
-
-        for g in range(GRP):
-            if g == ZG:
+            for g in ZG:
+                for k in range(3):
+                    lcopy(g, 2 * x + 1 - h, 4 + k, dev(x=xs[k])).wait_send()
+
+        for g in range(GRP):
+            if g in ZG:
                 continue
             for k in range(3):
 
@@ -535,7 +565,8 @@
             arrived(ER.at[g], er.at[g])
             for cc in range(2):
                 cols = slice(cc * HALF + GW * g, cc * HALF + GW * (g + 1))
-                rec_out[:, :, cols] = jnp.where(c == cc, E[g, :, own, :], ER[g])
+                RO[:, :, cols] = jnp.where(c == cc, E[g, :, own, :], ER[g])
+        pltpu.make_async_copy(RO, rec_out, osem.at[0]).start()
 
     def gcopy(n, k):
         to = xs[k]
@@ -612,30 +643,14 @@
             dst[...] = (E[g, t] - tg[t, :, cols]).astype(BF16)
         errors_first(g, sends)
 
-    def decoder_rest():
-        sends = []
-        count[0] = 0
-        for g in range(GRP):
-            exchange(g)
-        for g in range(GRP):
-            exchanged(g)
-            recon(g, sends)
-            error_block(g, sends)
-        gather_errors(sends)
-        grads()
-        recon_out()
-        line_sums(GN - GLAG)
-        for cp in sends:
-            cp.wait_send()
-        grads_drain()
-
     def encoder_rest():
         sends = []
-        for g in range(GRP):
-            exchange(g)
-        for g in range(GRP):
-            exchanged(g)
-            recon(g, sends)
+        for g in range(GRP + 2):
+            if g < GRP:
+                exchange(g)
+            if g >= 2:
+                exchanged(g - 2)
+                recon(g - 2, sends)
         recon_out()
         line_sums(0)
         for cp in sends:
@@ -644,10 +659,10 @@
     enter()
     pl.when(x == 0)(encode)
     pl.when(x > 0)(decode)
-    pl.when(x > 0)(decoder_rest)
     pl.when(x == 0)(encoder_rest)
     grads_out()
     exchange_drain()
+    pltpu.make_async_copy(RO, rec_out, osem.at[0]).wait()
 
 
 def body(sources, targets, blocks, enc_bias, token_code, feature_threshold_code, dec_map):
@@ -661,7 +676,7 @@
             jax.ShapeDtypeStruct((2, 48, 2048), BF16),
         ),
         in_specs=[pl.BlockSpec(memory_space=pltpu.SMEM), vm, vm, pl.BlockSpec(memory_space=pl.ANY), vm, vm, vm],
-        out_specs=(vm, vm),
+        out_specs=(pl.BlockSpec(memory_space=pl.ANY), vm),
         scratch_shapes=[
             V((2048, 4608), BF16),
             V((2, GRP, 2, 4, ROWS, GW), BF16),
@@ -683,8 +698,12 @@
             V((8, ROWS, GW), BF16),
             V((8, ROWS, GW), BF16),
             V((8, ROWS, GW), BF16),
+            V((8, ROWS, GW), BF16),
+            V((8, ROWS, GW), BF16),
+            V((8, ROWS, GW), BF16),
             V((GRP, 4, ROWS, GW), F32),
             V((GRP, 4, 24, GW), F32),
+            V((4, 24, 4608), F32),
             V((GN, 8, ROWS, GC), BF16),
             V((GN, 4, 2, ROWS, GC), BF16),
             V((GN, 2, ROWS, GC), F32),
@@ -692,7 +711,7 @@
             V((GN, 2, ROWS, GC), BF16),
             D((NCH,)),
             D((4,)),
-            D((64,)),
+            D((128,)),
             D((GRP, 2, 4, 2)),
             D((GRP, 2, 4)),
             D((2, 2, NCH, 2)),
@@ -712,6 +731,7 @@
             D((GN, 4)),
             D((GN,)),
             D((GN,)),
+            D((1,)),
         ],
         compiler_params=pltpu.CompilerParams(
             collective_id=1, has_side_effects=True, vmem_limit_bytes=62 * 2**20

time: 142 us -> 138 us (0.972)
  Pallas kernels: 137 us -> 133 us
    pallas_call x1, Pallas kernels: 137 us -> 133 us  [body(): pl.pallas_call(kernel, out_shape=(jax.ShapeDtypeStruct((4, 24, 4608), F32...]
where the time goes in v3:
time: 138 us
  Pallas kernels  133 us (96%)
  other arithmetic  2.9 us (2%)
    pallas_call x1, Pallas kernels, body(): pl.pallas_call(kernel, out_shape=(jax.ShapeDtypeStruct((4, 24, 4608), F32...  133 us
    sub x1, other arithmetic, body(): return (recon - targets.astype(F32), pre_grads)  2.9 us

profile of v3, /device:TPU:1, one launch (start us, length us, event | category | flops | bytes accessed | tf_op | source)
XLA Modules:
  0.0 137.8 jit_solution(536859518217738133)
XLA Ops:
  0.6 0.0 copy-start
  0.6 133.5 %transcoder.1 = (f32[4,24,4608]{2,1,0:T(8,128)}, bf16[2,48,2048]{2,1,0:T(8,128)(2,1)}) custom-call(s32[6]{0:T(128)} %dm.1, bf16[2,24,4608]{2,1,0:T(8,128)(2,1)} %src.1, bf16[4,24,4608]{2,1,0:T(8,128)(2,1)} %tgt.1, bf16[1,2048,4608]{2,1,0:T(8,128)(2,1)} %w_hbm.1, f32[2,2048]{1,0:T(2,128)} %bias.1, s32[2,384]{1,0:T(2,128)} %tok.1, s32[2,2048]{1,0:T(2,128)} %fc.1), custom_call_target="tpu_custom_call" | custom-call | tf_op jit(solution)/shard_map/transcoder/pallas_call | solution.py:672
  134.1 0.0 copy-done
  134.1 0.0 copy-start.1
  134.1 2.9 %convert_subtract_fusion = f32[4,24,4608]{2,1,0:T(8,128)} fusion(f32[4,24,4608]{2,1,0:T(8,128)} %get-tuple-element.4, bf16[4,24,4608]{2,1,0:T(8,128)(2,1)S(1)} %copy-done), kind=kLoop, calls=%fused_computation | loop fusion | flops 884736 | bytes 4423680 | tf_op jit(solution)/shard_map/sub | solution.py:741
  137.0 0.0 copy-done.1
  137.0 0.7 copy.10
Async XLA Ops:
  0.6 133.5 %copy-start = (bf16[4,24,4608]{2,1,0:T(8,128)(2,1)S(1)}, bf16[4,24,4608]{2,1,0:T(8,128)(2,1)}, u32[]{:S(2)}) copy-start(bf16[4,24,4608]{2,1,0:T(8,128)(2,1)} %tgt.1) | copy-start | bytes 2654212
  134.1 2.9 %copy-start.1 = (bf16[2,48,2048]{2,1,0:T(8,128)(2,1)S(1)}, bf16[2,48,2048]{2,1,0:T(8,128)(2,1)}, u32[]{:S(2)}) copy-start(bf16[2,48,2048]{2,1,0:T(8,128)(2,1)} %get-tuple-element.9) | copy-start | bytes 1179652

commit v4 on v3

--- a/solution.py
+++ b/solution.py
@@ -95,6 +95,7 @@
         v = src[...].astype(F32)
         sx_send[...] = half_of(v, o)
         sx[:, own, :] = half_of(v, c)
+        codes()
         pl.semaphore_wait(bar, len(peers))
 
     def sources_in(sends):
@@ -273,8 +274,6 @@
             X[c, g, l, y] = sx[h, :, cols].astype(BF16)
             XO[g] = sx[1 - h, :, cols].astype(BF16)
             gather_first(g, sends)
-        targets_out(sends)
-        codes()
         gather_own(sends)
         line = (dev(x=1), dev(x=3))
 
@@ -309,6 +308,7 @@
             return 0
 
         lax.fori_loop(0, NCH, chunk, 0)
+        targets_out(sends)
         gather_rest(sends)
         lax.fori_loop(NCH, STEPS, chunk, 0)
 
@@ -360,7 +360,6 @@
         xin = []
         sources_in(xin)
         targets_out(xin)
-        codes()
         nxt = (dev(x=lax.rem(x + 1, 4)), dev(x=lax.rem(x + 3, 4)))
         more = (x < 3, x > 1)
         lag = ((x - 1) * LH, (3 - x) * LH)

time: 138 us -> 140 us (1.014)
  Pallas kernels: 133 us -> 136 us
    pallas_call x1, Pallas kernels: 133 us -> 136 us  [body(): pl.pallas_call(kernel, out_shape=(jax.ShapeDtypeStruct((4, 24, 4608), F32...]
where the time goes in v4:
time: 140 us
  Pallas kernels  136 us (97%)
  other arithmetic  2.9 us (2%)
    pallas_call x1, Pallas kernels, body(): pl.pallas_call(kernel, out_shape=(jax.ShapeDtypeStruct((4, 24, 4608), F32...  136 us
    sub x1, other arithmetic, body(): return (recon - targets.astype(F32), pre_grads)  2.9 us

profile of v4, /device:TPU:1, one launch (start us, length us, event | category | flops | bytes accessed | tf_op | source)
XLA Modules:
  0.0 140.0 jit_solution(10891631283875662600)
XLA Ops:
  0.6 0.0 copy-start
  0.6 135.6 %transcoder.1 = (f32[4,24,4608]{2,1,0:T(8,128)}, bf16[2,48,2048]{2,1,0:T(8,128)(2,1)}) custom-call(s32[6]{0:T(128)} %dm.1, bf16[2,24,4608]{2,1,0:T(8,128)(2,1)} %src.1, bf16[4,24,4608]{2,1,0:T(8,128)(2,1)} %tgt.1, bf16[1,2048,4608]{2,1,0:T(8,128)(2,1)} %w_hbm.1, f32[2,2048]{1,0:T(2,128)} %bias.1, s32[2,384]{1,0:T(2,128)} %tok.1, s32[2,2048]{1,0:T(2,128)} %fc.1), custom_call_target="tpu_custom_call" | custom-call | tf_op jit(solution)/shard_map/transcoder/pallas_call | solution.py:671
  136.3 0.0 copy-done
  136.3 0.0 copy-start.1
  136.3 2.9 %convert_subtract_fusion = f32[4,24,4608]{2,1,0:T(8,128)} fusion(f32[4,24,4608]{2,1,0:T(8,128)} %get-tuple-element.4, bf16[4,24,4608]{2,1,0:T(8,128)(2,1)S(1)} %copy-done), kind=kLoop, calls=%fused_computation | loop fusion | flops 884736 | bytes 4423680 | tf_op jit(solution)/shard_map/sub | solution.py:740
  139.2 0.0 copy-done.1
  139.2 0.7 copy.10
Async XLA Ops:
  0.6 135.7 %copy-start = (bf16[4,24,4608]{2,1,0:T(8,128)(2,1)S(1)}, bf16[4,24,4608]{2,1,0:T(8,128)(2,1)}, u32[]{:S(2)}) copy-start(bf16[4,24,4608]{2,1,0:T(8,128)(2,1)} %tgt.1) | copy-start | bytes 2654212
  136.3 2.9 %copy-start.1 = (bf16[2,48,2048]{2,1,0:T(8,128)(2,1)S(1)}, bf16[2,48,2048]{2,1,0:T(8,128)(2,1)}, u32[]{:S(2)}) copy-start(bf16[2,48,2048]{2,1,0:T(8,128)(2,1)} %get-tuple-element.9) | copy-start | bytes 1179652
